TPU v7x, 32 devices: a whole 2x2x4 slice. The times are simulated.
32 devices in a mesh: ctx: 4 (over y, core), head: 8 (over z, x).
Axes of the slice: x: 2, y: 2, z: 4, core: 2. Of those that a mesh axis runs over, the one named last changes fastest.
Arguments:
- conv_input: bfloat16 [8192, 20480], P(('ctx', 'head')), may hold values from -6 to 6
- dt_raw: bfloat16 [8192, 256], P(('ctx', 'head')), as said below
- conv_weight: bfloat16 [4, 20480], replicated, may hold values from -3 to 3
- conv_bias: float32 [20480], replicated, may hold values from -3 to 3
- a_log: float32 [256], replicated, may hold values from -0.2 to 0.2
- dt_bias: float32 [256], replicated, as said below
- d_skip: float32 [256], replicated, may hold values from 0.5 to 1.5
Outputs:
- scan_out: bfloat16 [8192, 16384], P('ctx', 'head')
Inputs may be any that keep to these rules, and one draw needn't show every extreme that they name: softplus(dt_bias[h]) lies between 0.02 / 8192 and 0.04 for every head. softplus(dt_raw[t, h] + dt_bias[h]) lies between 0.02 / 8192 and 0.5 for every token and head.
All inputs are finite; a program needn't handle non-finite values.
Results may differ from a plain program's by a relative error of at most 0.0046.
Values may be sent and summed in bfloat16 or wider, within the bound.
A program may use at most 256 MiB of HBM per device.

v0:
```python
import jax
import jax.numpy as jnp
from jax import lax
from jax.sharding import PartitionSpec as P

HEADS = 256
HEADDIM = 64
STATE = 256
GROUPS = 8
CONV = 4
SPAN = 512


def shifted(value, axis, by):
    size = lax.axis_size(axis)
    pairs = [(i, i + by) for i in range(size) if 0 <= i + by < size]
    return lax.ppermute(value, axis, pairs)


def prefix(value, axis, combine, identity):
    size, position = (lax.axis_size(axis), lax.axis_index(axis))
    everything = jax.tree.map(lambda part: lax.all_gather(part, axis), value)
    start = jax.tree.map(
        lambda part, zero: jnp.broadcast_to(jnp.asarray(zero, part.dtype), part.shape),
        value,
        identity,
    )

    def turn(k, before):
        reached = k < position
        new = combine(before, jax.tree.map(lambda part: part[k], everything))
        return jax.tree.map(lambda a, b: jnp.where(reached, a, b), new, before)

    return lax.fori_loop(0, size, turn, start)


def compose(earlier, later):
    fade = jnp.exp(jnp.repeat(later[1], HEADDIM, axis=-1))
    return (earlier[0] * fade[..., None, :] + later[0], earlier[1] + later[1])


def on_device(conv_input, dt_raw, conv_weight, conv_bias, a_log, dt_bias, d_skip):
    f32 = jnp.float32
    head_count = lax.axis_size("head")
    heads_dev = HEADS // head_count
    repeat_count = head_count // GROUPS
    head_pos = lax.axis_index("head")
    group = head_pos // repeat_count
    rows = conv_input.shape[0]
    x_width = HEADS * HEADDIM
    slab = heads_dev * HEADDIM
    x_part = conv_input[:, :x_width].reshape(rows, head_count, slab)
    step_part = dt_raw.reshape(rows, head_count, heads_dev)
    arrived, steps = (
        lax.all_to_all(x_part, "head", split_axis=1, concat_axis=0, tiled=True),
        lax.all_to_all(step_part, "head", split_axis=1, concat_axis=0, tiled=True),
    )
    length = arrived.shape[0]
    shared = lax.all_gather(conv_input[:, x_width:], "head", axis=0, tiled=True)
    b_cols = lax.dynamic_slice_in_dim(shared, group * STATE, STATE, 1)
    c_cols = lax.dynamic_slice_in_dim(shared, (GROUPS + group) * STATE, STATE, 1)
    local = jnp.concatenate([arrived.reshape(length, slab), b_cols, c_cols], 1)
    steps = steps.reshape(length, heads_dev)

    def columns(table):
        last = table.ndim - 1
        return jnp.concatenate(
            [
                lax.dynamic_slice_in_dim(table, head_pos * slab, slab, last),
                lax.dynamic_slice_in_dim(table, x_width + group * STATE, STATE, last),
                lax.dynamic_slice_in_dim(table, x_width + (GROUPS + group) * STATE, STATE, last),
            ],
            last,
        )

    kernel = columns(conv_weight).astype(f32)
    offset = columns(conv_bias)
    rim = shifted(local[length - (CONV - 1) :], "ctx", 1)
    padded = jnp.concatenate([rim, local], 0)
    total = padded[0:length].astype(f32) * kernel[0]
    for k in range(1, CONV):
        total = total + padded[k : k + length].astype(f32) * kernel[k]
    act = jax.nn.silu(total + offset).astype(jnp.bfloat16)
    rate = -jnp.exp(lax.dynamic_slice_in_dim(a_log, head_pos * heads_dev, heads_dev, 0))
    bias = lax.dynamic_slice_in_dim(dt_bias, head_pos * heads_dev, heads_dev, 0)
    skip = jnp.repeat(lax.dynamic_slice_in_dim(d_skip, head_pos * heads_dev, heads_dev, 0), HEADDIM)
    step = jax.nn.softplus(steps.astype(f32) + bias)
    blocks = length // SPAN
    x_blocks = act[:, :slab].reshape(blocks, SPAN, slab)
    b_blocks = act[:, slab : slab + STATE].reshape(blocks, SPAN, STATE)
    c_blocks = act[:, slab + STATE :].reshape(blocks, SPAN, STATE)
    step_blocks = step.reshape(blocks, SPAN, heads_dev)
    cum = jnp.cumsum((rate * step).reshape(blocks, SPAN, heads_dev), axis=1)
    tri = lax.broadcasted_iota(jnp.int32, (SPAN, SPAN), 0) >= lax.broadcasted_iota(
        jnp.int32, (SPAN, SPAN), 1
    )

    def local_block(state, inputs):
        x_now, b_now, c_now, step_now, cum_now = inputs
        gram = jnp.dot(c_now, b_now.T, preferred_element_type=f32)
        cum_t = cum_now.T
        decay = jnp.exp(jnp.where(tri[None], cum_t[:, :, None] - cum_t[:, None, :], -jnp.inf))
        mix = (gram[None] * decay * step_now.T[:, None, :]).astype(jnp.bfloat16)
        x_heads = x_now.reshape(SPAN, heads_dev, HEADDIM)
        y_block = jnp.einsum("hts,shp->thp", mix, x_heads, preferred_element_type=f32).reshape(
            SPAN, slab
        )
        weight = jnp.exp(cum_now[-1][None, :] - cum_now) * step_now
        xw = (x_heads.astype(f32) * weight[:, :, None]).astype(jnp.bfloat16).reshape(SPAN, slab)
        contrib = jnp.einsum("sn,sc->nc", b_now, xw, preferred_element_type=f32)
        fade = jnp.exp(jnp.repeat(cum_now[-1], HEADDIM))
        return (state * fade[None, :] + contrib, (y_block, state))

    start_state = jnp.zeros((STATE, slab), f32)
    final, (y_blocks, entering) = lax.scan(
        local_block, start_state, (x_blocks, b_blocks, c_blocks, step_blocks, cum)
    )
    block_totals = cum[:, -1, :]
    totals = jnp.sum(block_totals, axis=0)
    incoming, passed = prefix(
        (final, totals),
        "ctx",
        compose,
        (jnp.zeros((STATE, slab), f32), jnp.zeros((heads_dev,), f32)),
    )
    before = jnp.concatenate(
        [jnp.zeros((1, heads_dev), f32), jnp.cumsum(block_totals, axis=0)[:-1]], 0
    )
    carried = jnp.exp(jnp.repeat(before, HEADDIM, axis=1))[:, None, :] * incoming[None]
    full_state = entering + carried
    grown = jnp.exp(jnp.repeat(cum, HEADDIM, axis=2))
    y_state = grown * jnp.einsum(
        "bqn,bnc->bqc", c_blocks.astype(f32), full_state, precision=lax.Precision.HIGHEST
    )
    result = y_blocks + y_state + skip * x_blocks.astype(f32)
    return result.astype(jnp.bfloat16).reshape(length, slab)


def solution(mesh):
    placed = (P(("ctx", "head"), None), P(("ctx", "head"), None), P(), P(), P(), P(), P())
    return jax.shard_map(
        on_device, mesh=mesh, in_specs=placed, out_specs=P("ctx", "head"), check_vma=False
    )
```

profile of v0, /device:TPU:23, one launch (start us, length us, event | category | flops | bytes accessed | tf_op | source)
XLA Modules:
  0.0 725.4 jit_solution(6228106980799238935)
XLA Ops:
  11.4 5.5 all-to-all-start
  16.9 8.7 %slice.58 = bf16[256,16384]{1,0:T(8,128)(2,1)} slice(bf16[256,20480]{1,0:T(8,128)(2,1)} %param.11), slice={[0:256], [0:16384]} | slice | bytes 16777216 | tf_op jit(solution)/shard_map/slice | solution.py:52
  25.6 11.9 %copy.52 = bf16[256,16384]{0,1:T(8,128)(2,1)} copy(bf16[256,16384]{1,0:T(8,128)(2,1)} %slice.58) | data formatting | bytes 16777216
  37.6 11.4 %copy.43 = bf16[256,8,2048]{2,0,1:T(8,128)(2,1)} copy(bf16[256,8,2048]{0,2,1:T(8,128)(2,1)} %bitcast.112) | data formatting | bytes 16777216 | tf_op jit(solution)/shard_map/reshape | solution.py:52
  49.0 5.6 all-to-all-start.1
  59.4 4.6 reduce-window.6
  64.8 340.2 %all-gather.5.cloned.1.call-done = bf16[2048,4096]{1,0:T(8,128)(2,1)} async-done(((bf16[256,4096]{1,0:T(8,128)(2,1)}), bf16[2048,4096]{1,0:T(8,128)(2,1)}) %all-gather.5.cloned.1.call-update) | async-done | bytes 16777232 | tf_op jit(solution)/shard_map/all_gather | solution.py:59
  407.7 7.5 %pad_maximum_fusion = bf16[2048,2560]{1,0:T(8,128)(2,1)S(1)} fusion(bf16[2048,256]{1,0:T(8,128)(2,1)} %get-tuple-element.291, bf16[2048,256]{1,0:T(8,128)(2,1)S(1)} %get-tuple-element.290, bf16[2048,2048]{1,0:T(8,128)(2,1)} %bitcast.8), kind=kLoop, calls=%fused_computation.33 | loop fusion | flops 31457280 | bytes 20971520 | tf_op jit(solution)/shard_map/concatenate | solution.py:62
  418.3 7.1 maximum_maximum_fusion
  425.4 19.6 %multiply_convert_fusion.3 = bf16[2048,2560]{1,0:T(8,128)(2,1)} fusion(bf16[2051,2560]{1,0:T(8,128)(2,1)S(1)} %maximum_maximum_fusion, f32[2560]{0:T(1024)S(1)} %pad_maximum_fusion.1, f32[2560]{0:T(1024)S(1)} %get-tuple-element.255, f32[2560]{0:T(1024)S(1)} %get-tuple-element.256, f32[2560]{0:T(1024)S(1)} %get-tuple-element.257, ...), kind=kLoop, calls=%fused_computation.30 | loop fusion | flops 115343360 | bytes 52480000 | tf_op jit(solution)/shard_map/convert_element_type | solution.py:83
  445.0 8.4 %slice.85 = bf16[2048,2048]{1,0:T(8,128)(2,1)} slice(bf16[2048,2560]{1,0:T(8,128)(2,1)} %multiply_convert_fusion.3), slice={[0:2048], [0:2048]} | slice | bytes 16777216 | tf_op jit(solution)/shard_map/slice | solution.py:89
  456.5 161.2 %while.29 = (s32[]{:T(128)}, f32[256,2048]{1,0:T(8,128)S(1)}, f32[4,512,2048]{2,1,0:T(8,128)}, f32[4,256,2048]{2,1,0:T(8,128)}, f32[4,512,32]{1,2,0:T(8,128)S(1)...) while((s32[]{:T(128)}, f32[256,2048]{1,0:T(8,128)S(1)}, ...), condition=%wide.region_3.4_spmd.clone, body=%wide.region_2.3_spmd.clone.sunk | while | flops 1792311296 | bytes 50367904 | solution.py:115
  462.6 3.9 copy.70
  466.6 11.8 %fusion.43 = f32[32,64,512]{2,1,0:T(8,128)} fusion(bf16[512,32,64]{0,2,1:T(8,128)(2,1)} %bitcast.106, f32[32,512]{1,0:T(8,128)S(1)} %get-tuple-element.381, f32[32,512]{1,0:T(8,128)} %get-tuple-element.382, f32[512,512]{1,0:T(8,128)S(1)} %fusion.42, pred[512,512]{1,0:T(8,128)(4,1)S(1)} %iota_compare_fusion.2), kind=kOutput, calls=%fused_computation.5.clone.1 | convolution fusion | flops 1115684864 | bytes 7733248 | tf_op jit(solution)/shard_map/while/body/eval_jaxpr/hts,shp->thp/dot_general | solution.py:105
  478.4 5.4 copy.71
  483.8 4.6 constant_dynamic-update-slice_fusion.2
  502.9 3.9 copy.70
  506.9 11.8 %fusion.43 = f32[32,64,512]{2,1,0:T(8,128)} fusion(bf16[512,32,64]{0,2,1:T(8,128)(2,1)} %bitcast.106, f32[32,512]{1,0:T(8,128)S(1)} %get-tuple-element.381, f32[32,512]{1,0:T(8,128)} %get-tuple-element.382, f32[512,512]{1,0:T(8,128)S(1)} %fusion.42, pred[512,512]{1,0:T(8,128)(4,1)S(1)} %iota_compare_fusion.2), kind=kOutput, calls=%fused_computation.5.clone.1 | convolution fusion | flops 1115684864 | bytes 7733248 | tf_op jit(solution)/shard_map/while/body/eval_jaxpr/hts,shp->thp/dot_general | solution.py:105
  518.7 5.4 copy.71
  524.1 4.7 constant_dynamic-update-slice_fusion.2
  547.2 11.8 %fusion.43 = f32[32,64,512]{2,1,0:T(8,128)} fusion(bf16[512,32,64]{0,2,1:T(8,128)(2,1)} %bitcast.106, f32[32,512]{1,0:T(8,128)S(1)} %get-tuple-element.381, f32[32,512]{1,0:T(8,128)} %get-tuple-element.382, f32[512,512]{1,0:T(8,128)S(1)} %fusion.42, pred[512,512]{1,0:T(8,128)(4,1)S(1)} %iota_compare_fusion.2), kind=kOutput, calls=%fused_computation.5.clone.1 | convolution fusion | flops 1115684864 | bytes 7733248 | tf_op jit(solution)/shard_map/while/body/eval_jaxpr/hts,shp->thp/dot_general | solution.py:105
  559.0 5.4 copy.71
  564.4 4.7 constant_dynamic-update-slice_fusion.2
  587.5 11.8 %fusion.43 = f32[32,64,512]{2,1,0:T(8,128)} fusion(bf16[512,32,64]{0,2,1:T(8,128)(2,1)} %bitcast.106, f32[32,512]{1,0:T(8,128)S(1)} %get-tuple-element.381, f32[32,512]{1,0:T(8,128)} %get-tuple-element.382, f32[512,512]{1,0:T(8,128)S(1)} %fusion.42, pred[512,512]{1,0:T(8,128)(4,1)S(1)} %iota_compare_fusion.2), kind=kOutput, calls=%fused_computation.5.clone.1 | convolution fusion | flops 1115684864 | bytes 7733248 | tf_op jit(solution)/shard_map/while/body/eval_jaxpr/hts,shp->thp/dot_general | solution.py:105
  599.3 5.4 copy.71
  604.7 4.6 constant_dynamic-update-slice_fusion.2
  621.0 7.7 %all-reduce.1 = f32[128]{0:T(128)S(1)} all-reduce(f32[128]{0:T(128)S(1)} %dynamic-update-slice), channel_id=2, replica_groups=mesh['ctx'=4,'head'=8] {'ctx'}, use_global_device_ids=true, to_apply=%add.1 | all-reduce | flops 128 | bytes 1024
  630.1 9.2 %broadcast_in_dim.63 = f32[4,512,32,64]{1,3,2,0:T(8,128)} broadcast(f32[4,512,32]{1,2,0:T(8,128)S(1)} %fusion.23), dimensions={0,1,2} | broadcast | bytes 17039360 | tf_op jit(solution)/shard_map/broadcast_in_dim | solution.py:131
  639.3 16.5 %copy.46 = f32[4,512,2048]{2,1,0:T(8,128)} copy(f32[4,512,2048]{1,2,0:T(8,128)} %bitcast.111) | data formatting | bytes 33554432 | tf_op jit(solution)/shard_map/exp | solution.py:131
  655.8 24.6 %all-gather.7.cloned.1.call-done = f32[1024,2048]{1,0:T(8,128)} async-done(((f32[256,2048]{1,0:T(8,128)}), f32[1024,2048]{1,0:T(8,128)}) %all-gather.7.cloned.1.call-update) | async-done | bytes 8388624 | tf_op jit(solution)/shard_map/all_gather | solution.py:22
  680.3 14.6 %while.30 = (s32[]{:T(128)}, f32[256,2048]{1,0:T(8,128)S(1)}, s32[]{:T(128)}, f32[4,32]{1,0:T(4,128)S(1)}, f32[4,256,2048]{2,1,0:T(8,128)}, /*index=5*/s32[]{:T(128)}, s32[]{:T(128)}) while((s32[]{:T(128)}, f32[256,2048]{1,0:T(8,128)S(1)}, s32[]{:T(128)}, f32[4,32]{1,0:T(4,128)S(1)}, f32[4,256,2048]{2,1,0:T(8,128)}, ...), condition=%wide.region_7.8_spmd.clone, body=%wide.region_6.7_spmd.clone.sunk | while | flops 2097156 | bytes 6324713 | solution.py:34
  694.9 23.6 %add_convert_fusion = bf16[4,512,2048]{2,1,0:T(8,128)(2,1)} fusion(bf16[4,512,2048]{2,1,0:T(8,128)(2,1)} %get-tuple-element.449, f32[4,512,2048]{2,1,0:T(8,128)} %get-tuple-element.153, f32[4,512,2048]{2,1,0:T(8,128)} %copy.46, f32[2048]{0:T(1024)S(1)} %mul.190, bf16[4,512,256]{2,1,0:T(8,128)(2,1)S(1)} %copy-done.2, ...), kind=kOutput, calls=%fused_computation.31 | convolution fusion | flops 12914262016 | bytes 61906944 | tf_op jit(solution)/shard_map/bqn,bnc->bqc/dot_general | solution.py:132
  (141 shorter events, 103.8 us)
Async XLA Ops:
  6.5 398.5 %all-gather.5.cloned.1.call-start = ((), (), s32[]{:S(2)}) async-start(), calls=%async_computation.2 | async-start | bytes 18874368 | tf_op jit(solution)/shard_map/all_gather | solution.py:59
  11.4 37.6 %all-to-all-start = ((bf16[256,8,32]{0,2,1:T(8,128)(2,1)}), bf16[256,8,32]{0,2,1:T(8,128)(2,1)S(1)}, u32[]{:S(2)}, u32[]{:S(2)}) async-start(bf16[256,8,32]{0,2,1:T(8,128)(2,1)} %bitcast), calls=%async_computation | async-start | bytes 262144 | tf_op jit(solution)/shard_map/all_to_all | solution.py:56
  48.9 6.3 copy-start.7
  49.0 6.4 copy-start.8
  49.0 358.7 %all-to-all-start.1 = ((bf16[256,8,2048]{2,0,1:T(8,128)(2,1)}), bf16[256,8,2048]{2,0,1:T(8,128)(2,1)}, u32[]{:S(2)}, u32[]{:S(2)}) async-start(bf16[256,8,2048]{2,0,1:T(8,128)(2,1)} %copy.43), calls=%async_computation.1 | async-start | bytes 16777216 | tf_op jit(solution)/shard_map/all_to_all | solution.py:55
  54.5 625.8 %all-gather.7.cloned.1.call-start = ((), (), s32[]{:S(2)}) async-start(), calls=%async_computation.3 | async-start | bytes 10485760 | tf_op jit(solution)/shard_map/all_gather | solution.py:22
  64.1 0.7 copy-start.3
  64.8 351.9 %copy-start.5 = (f32[4,32,4]{1,2,0:T(4,128)}, f32[4,32,4]{1,2,0:T(4,128)S(1)}, u32[]{:S(2)}) copy-start(f32[4,32,4]{1,2,0:T(4,128)S(1)} %slice.75) | copy-start | bytes 6148
  407.7 9.0 %copy-start.4 = (f32[4,32,4,128]{3,1,2,0:T(8,128)S(1)}, f32[4,32,4,128]{3,1,2,0:T(8,128)}, u32[]{:S(2)}) copy-start(f32[4,32,4,128]{3,1,2,0:T(8,128)} %copy-done.3) | copy-start | bytes 786436
  407.7 10.6 %copy-start.1 = (bf16[2048,256]{1,0:T(8,128)(2,1)S(1)}, bf16[2048,256]{1,0:T(8,128)(2,1)}, u32[]{:S(2)}) copy-start(bf16[2048,256]{1,0:T(8,128)(2,1)} %get-tuple-element.291) | copy-start | bytes 3145732
  415.2 3.1 collective-permute-start
  456.4 162.6 %copy-start.9 = (f32[256]{0:T(256)S(1)}, f32[256]{0:T(256)}, u32[]{:S(2)}) copy-start(f32[256]{0:T(256)} %param.17) | copy-start | bytes 3076
  456.5 162.8 %copy-start.10 = (u32[32]{0:T(128)S(1)}, u32[32]{0:T(128)}, u32[]{:S(2)}) copy-start(u32[32]{0:T(128)} %constant.100) | copy-start | bytes 388
  456.5 172.5 %copy-start.6 = (f32[4,32,4]{1,2,0:T(4,128)S(1)}, f32[4,32,4]{1,2,0:T(4,128)}, u32[]{:S(2)}) copy-start(f32[4,32,4]{1,2,0:T(4,128)} %copy-done.5) | copy-start | bytes 6148
  617.6 1.3 copy-start
  680.3 14.6 %copy-start.2 = (bf16[4,512,256]{2,1,0:T(8,128)(2,1)S(1)}, bf16[4,512,256]{2,1,0:T(8,128)(2,1)}, u32[]{:S(2)}) copy-start(bf16[4,512,256]{2,1,0:T(8,128)(2,1)} %get-tuple-element.453) | copy-start | bytes 3145732
Sparse Core Ops, SparseCore 0:
  9.8 395.1 all-gather.4
  619.1 61.1 all-gather.6
where the time goes:
time: 731 us; the launch traced here: 725 us
  waiting for transfers between devices  366 us (50%)
  local copies, waits for them, and re-layouts  160 us (22%)
  matrix products  88.1 us (12%)
  other arithmetic  75.7 us (10%)
  between operations  14.2 us (2%)
  starting transfers between devices  12.6 us (2%)
  blocking collectives  7.67 us (1%)
    all_gather x1, waiting for transfers between devices, on_device(): shared = lax.all_gather(conv_input[:, x_width:], 'head', axis=0, tiled=True)  340 us
    dot_general x4, matrix products, local_block(): jnp.einsum('hts,shp->thp', mix, x_heads, preferred_element_type=f32)  47.1 us
    dynamic_update_slice x8, local copies, waits for them, and re-layouts, on_device(): lax.scan(local_block, start_state, (x_blocks, b_blocks, c_blocks, step_bl...  40 us
    dynamic_slice x12, local copies, waits for them, and re-layouts, on_device(): lax.scan(local_block, start_state, (x_blocks, b_blocks, c_blocks, step_bl...  32.3 us
    all_gather x1, waiting for transfers between devices, prefix(): everything = jax.tree.map(lambda part: lax.all_gather(part, axis), value)  24.6 us
    dot_general x1, matrix products, on_device(): jnp.einsum('bqn,bnc->bqc', c_blocks.astype(f32), full_state, precision=la...  23.6 us
    convert_element_type x1, other arithmetic, on_device(): act = jax.nn.silu(total + offset).astype(jnp.bfloat16)  19.6 us
    exp x1, local copies, waits for them, and re-layouts, on_device(): grown = jnp.exp(jnp.repeat(cum, HEADDIM, axis=2))  16.5 us
  transfers between devices with their start and end apart: 5, of which 3 were waited for; matrix products, arithmetic and copies ran while one was open for 10% of the time, Pallas kernels for 0%

commit v1 on v0

v1 whole, which is shorter than its diff:
```python
import functools

import jax
import jax.numpy as jnp
from jax import lax
from jax.experimental import pallas as pl
from jax.experimental.pallas import tpu as pltpu
from jax.sharding import PartitionSpec as P

HEADS = 256
HEADDIM = 64
STATE = 256
GROUPS = 8
CONV = 4
CHUNK = 128
UNIT = 256
RIM = 16
AHEAD = 3
SKIP_ROW = 126
TOTAL_ROW = 127

F32 = jnp.float32
BF16 = jnp.bfloat16
MESH = pl.DeviceIdType.MESH


def softplus(value):
    z = jnp.exp(-jnp.abs(value))
    s = z / (2.0 + z)
    q = s * s
    series = jnp.full_like(s, 1.0 / 15.0)
    for odd in (13, 11, 9, 7, 5, 3, 1):
        series = series * q + 1.0 / odd
    return jnp.maximum(value, 0.0) + 2.0 * s * series


def dot(a, b, precision=None):
    return jnp.dot(a, b, preferred_element_type=F32, precision=precision)


def kernel(
    n_ctx, n_head,
    x_hbm, dt_ref, w_ref, b_ref, head_ref,
    out_hbm,
    buf, dts, dtr, dtf, daf, b_t, c_act, gram, feat, fade_t, fade, e_u, e_v, e_g, y_buf, state, s_out, s_in,
    send_sem, recv_sem, dt_send, dt_recv, rim_send, rim_recv, chain_send, chain_recv, out_sem,
):
    tok = x_hbm.shape[0]
    length = tok * n_head
    slab = HEADS * HEADDIM // n_head
    hd = HEADS // n_head
    pieces = slab // UNIT
    per_unit = UNIT // HEADDIM
    x_width = HEADS * HEADDIM
    repeat_count = n_head // GROUPS
    n_chunk = length // CHUNK
    ctx = lax.axis_index("ctx")
    me = lax.axis_index("head")
    last = n_head - 1
    turns = sorted(range(1, n_head), key=lambda d: abs(2 * d - n_head))

    def device(c, j):
        return (c, j)

    barrier = pltpu.get_barrier_semaphore()

    def greet(c, j):
        pl.semaphore_signal(barrier, inc=1, device_id=device(c, j), device_id_type=MESH)

    for d in turns:
        greet(ctx, lax.rem(me + d, n_head))

    @pl.when(ctx < n_ctx - 1)
    def _():
        greet(ctx + 1, me)

        @pl.when(me == last)
        def _():
            for j in range(last):
                greet(ctx + 1, j)

    @pl.when(ctx > 0)
    def _():
        greet(ctx - 1, me)

        @pl.when(me < last)
        def _():
            greet(ctx - 1, last)

    def column(q, j):
        if isinstance(q, int) and q < 2:
            return pl.multiple_of(x_width + (q * GROUPS + j // repeat_count) * STATE, UNIT)
        return pl.multiple_of(j * slab + (q - 2) * UNIT, UNIT)

    def place(q):
        return pl.ds(pl.multiple_of(q * UNIT, UNIT), UNIT)

    def landing(q, src):
        return buf.at[pl.ds(pl.multiple_of(RIM + src * tok, RIM), tok), place(q)]

    def unit_copy(q, j):
        return pltpu.make_async_remote_copy(
            src_ref=x_hbm.at[:, pl.ds(column(q, j), UNIT)],
            dst_ref=landing(q, me),
            send_sem=send_sem.at[q, j],
            recv_sem=recv_sem.at[q, me],
            device_id=device(ctx, j),
            device_id_type=MESH,
        )

    def own_copy(q):
        return pltpu.make_async_copy(
            x_hbm.at[:, pl.ds(column(q, me), UNIT)], landing(q, me), recv_sem.at[q, me]
        )

    def unit_start(q):
        for d in turns:
            unit_copy(q, lax.rem(me + d, n_head)).start()
        own_copy(q).start()

    def unit_sent(q):
        for d in turns:
            unit_copy(q, lax.rem(me + d, n_head)).wait_send()

    def unit_arrived(q, src):
        pltpu.make_async_copy(landing(q, src), landing(q, src), recv_sem.at[q, src]).wait()

    def dt_copy(j):
        return pltpu.make_async_remote_copy(
            src_ref=dts.at[pl.ds(pl.multiple_of(j * hd, hd), hd), :],
            dst_ref=dtr.at[:, pl.ds(pl.multiple_of(me * tok, tok), tok)],
            send_sem=dt_send.at[j],
            recv_sem=dt_recv.at[me],
            device_id=device(ctx, j),
            device_id_type=MESH,
        )

    def rim_copy(part, j):
        start = column(part, j) if part < 2 else pl.multiple_of(j * slab, UNIT)
        size = UNIT if part < 2 else slab
        return pltpu.make_async_remote_copy(
            src_ref=x_hbm.at[pl.ds(tok - RIM, RIM), pl.ds(start, size)],
            dst_ref=buf.at[pl.ds(0, RIM), pl.ds(part * UNIT, size)],
            send_sem=rim_send.at[part, j],
            recv_sem=rim_recv.at[part],
            device_id=device(ctx + 1, j),
            device_id_type=MESH,
        )

    def rim_arrived(part):
        size = UNIT if part < 2 else slab
        where = buf.at[pl.ds(0, RIM), pl.ds(part * UNIT, size)]
        pltpu.make_async_copy(where, where, rim_recv.at[part]).wait()

    def chain_copy(p):
        return pltpu.make_async_remote_copy(
            src_ref=s_out.at[p],
            dst_ref=s_in.at[p],
            send_sem=chain_send.at[p],
            recv_sem=chain_recv.at[p],
            device_id=device(ctx + 1, me),
            device_id_type=MESH,
        )

    def out_copy(p):
        return pltpu.make_async_copy(
            buf.at[pl.ds(RIM, length), place(p + 2)], out_hbm.at[:, place(p)], out_sem.at[p]
        )

    dts[...] = dt_ref[...].astype(F32).T.astype(BF16)

    @pl.when(ctx == 0)
    def _():
        buf[0:RIM, :] = jnp.zeros((RIM, buf.shape[1]), BF16)
        s_in[...] = jnp.zeros(s_in.shape, F32)

    has_next = (ctx < n_ctx - 1).astype(jnp.int32)
    has_prev = (ctx > 0).astype(jnp.int32)
    is_last = (me == last).astype(jnp.int32)
    pl.semaphore_wait(
        barrier, last + has_next * (1 + last * is_last) + has_prev * (2 - is_last)
    )

    for d in turns:
        dt_copy(lax.rem(me + d, n_head)).start()
    own_dt = pltpu.make_async_copy(
        dts.at[pl.ds(pl.multiple_of(me * hd, hd), hd), :],
        dtr.at[:, pl.ds(pl.multiple_of(me * tok, tok), tok)],
        dt_recv.at[me],
    )
    own_dt.start()

    sends_rim = jnp.logical_and(ctx < n_ctx - 1, me == last)

    @pl.when(sends_rim)
    def _():
        for part in range(3):
            for j in range(n_head):
                rim_copy(part, j).start()

    unit_start(0)
    unit_start(1)
    for p in range(min(AHEAD, pieces)):
        unit_start(p + 2)

    for src in range(n_head):
        where = dtr.at[:, pl.ds(src * tok, tok)]
        pltpu.make_async_copy(where, where, dt_recv.at[src]).wait()
    mine = pl.ds(pl.multiple_of(me * hd, hd), hd)
    per_head = head_ref[mine, :]
    dt_now = softplus(dtr[...].astype(F32) + per_head[:, 1:2])
    dtf[...] = dt_now
    daf[...] = -jnp.exp(per_head[:, 0:1]) * dt_now
    upto = (
        lax.broadcasted_iota(jnp.int32, (CHUNK, CHUNK), 0)
        <= lax.broadcasted_iota(jnp.int32, (CHUNK, CHUNK), 1)
    ).astype(F32)
    lane = lax.broadcasted_iota(jnp.int32, (hd, 128), 1)

    def factors(k, carry):
        start, expo = carry
        span = pl.ds(pl.multiple_of(k * CHUNK, CHUNK), CHUNK)
        cum = dot(daf[:, span], upto, lax.Precision.HIGHEST)
        mid = cum[:, CHUNK // 2 - 1 : CHUNK // 2]
        end = cum[:, CHUNK - 1 : CHUNK]
        parts = []
        for value in (jnp.exp(cum - mid), jnp.exp(mid - cum) * dtf[:, span], jnp.exp(start + cum)):
            high = value.astype(BF16).astype(F32)
            parts += [high, value - high]
        zero = jnp.zeros((hd, CHUNK), F32)
        feat[span, :] = jnp.concatenate(parts + [zero, zero], 0).T.astype(BF16)
        expo = expo + jnp.where(lane == k, end - mid, 0.0)
        expo = expo + jnp.where(lane == k - 1, mid, 0.0)
        expo = expo + jnp.where(lane == TOTAL_ROW, end, 0.0)
        return start + end, expo

    _, expo = lax.fori_loop(
        0, n_chunk, factors, (jnp.zeros((hd, 1), F32), jnp.zeros((hd, 128), F32))
    )
    fade_t[...] = jnp.where(lane == SKIP_ROW, per_head[:, 2:3], jnp.exp(expo)).T

    def conv(q, start, src):
        cols = pl.ds(start, UNIT)
        taps = w_ref[:, cols].astype(F32)
        window = buf[pl.ds(pl.multiple_of(src * tok, RIM), tok + RIM), place(q)].astype(F32)
        first = RIM - (CONV - 1)
        total = window[first : first + tok] * taps[0:1]
        for k in range(1, CONV):
            total = total + window[first + k : first + k + tok] * taps[k : k + 1]
        total = total + b_ref[:, cols]
        return (total / (1.0 + jnp.exp(-total))).astype(BF16)

    @pl.when(ctx > 0)
    def _():
        for part in range(3):
            rim_arrived(part)

    causal = lax.broadcasted_iota(jnp.int32, (CHUNK, CHUNK), 0) >= lax.broadcasted_iota(
        jnp.int32, (CHUNK, CHUNK), 1
    )

    def projections(src, _):
        unit_arrived(0, src)
        unit_arrived(1, src)
        b_now = conv(0, column(0, me), src)
        c_now = conv(1, column(1, me), src)
        rows = pl.ds(pl.multiple_of(src * tok, tok), tok)
        b_t[:, rows] = b_now.astype(F32).T.astype(BF16)
        c_act[rows, :] = c_now
        for i in range(tok // CHUNK):
            part = slice(i * CHUNK, (i + 1) * CHUNK)
            inner = lax.dot_general(
                c_now[part], b_now[part], (((1,), (1,)), ((), ())), preferred_element_type=F32
            )
            gram[pl.ds(pl.multiple_of(src * tok + i * CHUNK, CHUNK), CHUNK), :] = jnp.where(
                causal, inner, 0.0
            ).astype(BF16)
        return 0

    lax.fori_loop(0, n_head, projections, 0)
    unit_sent(0)
    unit_sent(1)

    row = lax.broadcasted_iota(jnp.int32, (8 * hd, UNIT), 0)
    col = lax.broadcasted_iota(jnp.int32, (8 * hd, UNIT), 1) // HEADDIM

    def spread(p, at):
        head = col + p * per_unit
        hit = jnp.logical_or(row == head + at * hd, row == head + (at + 1) * hd)
        return jnp.where(hit, 1.0, 0.0).astype(BF16)

    def finish(p):
        @pl.when(ctx > 0)
        def _():
            pltpu.make_async_copy(s_in.at[p], s_in.at[p], chain_recv.at[p]).wait()

        slot = lax.rem(p, 2)

        @pl.when(jnp.logical_and(ctx > 0, ctx < n_ctx - 1))
        def _():
            s_out[p] = fade[slot, TOTAL_ROW : TOTAL_ROW + 1, :] * s_in[p] + s_out[p]
            chain_copy(p).start()

        e_g[...] = spread(p, 4)

        def block(i, _):
            rows = pl.ds(pl.multiple_of(i * tok, tok), tok)
            grown = dot(feat[rows, :], e_g[...])
            late = grown * dot(c_act[rows, :], s_in[p].astype(BF16))
            buf[pl.ds(pl.multiple_of(RIM + i * tok, RIM), tok), place(p + 2)] = (
                y_buf[slot, rows, :] + late
            ).astype(BF16)
            return 0

        lax.fori_loop(0, n_head, block, 0)
        out_copy(p).start()

    def piece(p, _):
        unit_sent(p + 2)

        @pl.when(p + AHEAD < pieces)
        def _():
            unit_start(p + AHEAD + 2)

        slot = lax.rem(p, 2)
        e_u[...] = spread(p, 0)
        e_v[...] = spread(p, 2)
        expand = jnp.where(row[0:hd] == col[0:hd] + p * per_unit, 1.0, 0.0)
        fade[slot] = dot(fade_t[...], expand, lax.Precision.HIGHEST)
        state[...] = jnp.zeros(state.shape, F32)

        def block(src, _):
            unit_arrived(p + 2, src)
            act = conv(p + 2, column(p + 2, me), src).astype(F32)
            rows = pl.ds(pl.multiple_of(src * tok, tok), tok)
            grow = dot(feat[rows, :], e_u[...])
            scaled = (act * dot(feat[rows, :], e_v[...])).astype(BF16)
            for i in range(tok // CHUNK):
                part = slice(i * CHUNK, (i + 1) * CHUNK)
                span = pl.ds(pl.multiple_of(src * tok + i * CHUNK, CHUNK), CHUNK)
                entering = state[...]
                y = dot(gram[span, :], scaled[part]) + dot(c_act[span, :], entering.astype(BF16))
                y_buf[slot, span, :] = (
                    grow[part] * y + fade[slot, SKIP_ROW : SKIP_ROW + 1, :] * act[part]
                )
                added = dot(b_t[:, span], scaled[part])
                k = src * (tok // CHUNK) + i
                state[...] = fade[slot, pl.ds(k, 1), :] * (entering + added)
            return 0

        lax.fori_loop(0, n_head, block, 0)
        s_out[p] = state[...]

        @pl.when(ctx == 0)
        def _():
            chain_copy(p).start()

        @pl.when(p > 0)
        def _():
            finish(p - 1)

        return 0

    lax.fori_loop(0, pieces, piece, 0)
    finish(pieces - 1)

    for d in turns:
        dt_copy(lax.rem(me + d, n_head)).wait_send()

    @pl.when(sends_rim)
    def _():
        for part in range(3):
            for j in range(n_head):
                rim_copy(part, j).wait_send()

    @pl.when(ctx < n_ctx - 1)
    def _():
        for p in range(pieces):
            chain_copy(p).wait_send()

    for p in range(pieces):
        out_copy(p).wait()


def on_device(conv_input, dt_raw, conv_weight, conv_bias, a_log, dt_bias, d_skip):
    n_ctx, n_head = lax.axis_size("ctx"), lax.axis_size("head")
    tok = conv_input.shape[0]
    length = tok * n_head
    slab = HEADS * HEADDIM // n_head
    hd = HEADS // n_head
    pieces = slab // UNIT
    per_head = jnp.stack([a_log, dt_bias, d_skip], 1)
    vmem = pl.BlockSpec(memory_space=pltpu.VMEM)
    anywhere = pl.BlockSpec(memory_space=pl.ANY)
    dma = pltpu.SemaphoreType.DMA
    return pl.pallas_call(
        functools.partial(kernel, n_ctx, n_head),
        out_shape=jax.ShapeDtypeStruct((length, slab), BF16),
        in_specs=[anywhere, vmem, vmem, vmem, vmem],
        out_specs=anywhere,
        scratch_shapes=[
            pltpu.VMEM((RIM + length, slab + 2 * STATE), BF16),
            pltpu.VMEM((HEADS, tok), BF16),
            pltpu.VMEM((hd, length), BF16),
            pltpu.VMEM((hd, length), F32),
            pltpu.VMEM((hd, length), F32),
            pltpu.VMEM((STATE, length), BF16),
            pltpu.VMEM((length, STATE), BF16),
            pltpu.VMEM((length, CHUNK), BF16),
            pltpu.VMEM((length, 8 * hd), BF16),
            pltpu.VMEM((128, hd), F32),
            pltpu.VMEM((2, 128, UNIT), F32),
            pltpu.VMEM((8 * hd, UNIT), BF16),
            pltpu.VMEM((8 * hd, UNIT), BF16),
            pltpu.VMEM((8 * hd, UNIT), BF16),
            pltpu.VMEM((2, length, UNIT), F32),
            pltpu.VMEM((STATE, UNIT), F32),
            pltpu.VMEM((pieces, STATE, UNIT), F32),
            pltpu.VMEM((pieces, STATE, UNIT), F32),
            dma((pieces + 2, n_head)),
            dma((pieces + 2, n_head)),
            dma((n_head,)),
            dma((n_head,)),
            dma((3, n_head)),
            dma((3,)),
            dma((pieces,)),
            dma((pieces,)),
            dma((pieces,)),
        ],
        compiler_params=pltpu.CompilerParams(
            collective_id=0, has_side_effects=True, vmem_limit_bytes=56 * 1024 * 1024
        ),
    )(conv_input, dt_raw, conv_weight, conv_bias.reshape(1, -1), per_head)


def solution(mesh):
    placed = (P(("ctx", "head"), None), P(("ctx", "head"), None), P(), P(), P(), P(), P())
    return jax.shard_map(
        on_device, mesh=mesh, in_specs=placed, out_specs=P("ctx", "head"), check_vma=False
    )
```

time: 731 us -> 268 us (0.37)
  waiting for transfers between devices: 366 us -> 0 us
  Pallas kernels: 0 us -> 257 us
  local copies, waits for them, and re-layouts: 160 us -> 9.24 us
  matrix products: 88.1 us -> 0 us
  other arithmetic: 75.7 us -> 0.72 us
  between operations: 14.2 us -> 0.01 us
  starting transfers between devices: 12.6 us -> 0 us
  blocking collectives: 7.67 us -> 0 us
    all_gather x2 -> x0, waiting for transfers between devices: 365 us -> none  [the longest x1 340 us: on_device(): shared = lax.all_gather(conv_input[:, x_width:], 'head', axis=0, tiled=True)]
    pallas_call x0 -> x1, Pallas kernels: none -> 257 us  [on_device(): pl.pallas_call(functools.partial(kernel, n_ctx, n_head), out_shape=jax.Sh...]
    dot_general x13 -> x0, matrix products: 88.1 us -> none  [the longest x4 47.1 us: local_block(): jnp.einsum('hts,shp->thp', mix, x_heads, preferred_element_type=f32)]
    dynamic_update_slice x8 -> x0, local copies, waits for them, and re-layouts: 40 us -> none  [on_device(): lax.scan(local_block, start_state, (x_blocks, b_blocks, c_blocks, step_bl...]
    dynamic_slice x19 -> x0, local copies, waits for them, and re-layouts: 38 us -> none  [the longest x12 32.3 us: on_device(): lax.scan(local_block, start_state, (x_blocks, b_blocks, c_blocks, step_bl...]
    convert_element_type x7 -> x0, other arithmetic: 33.3 us -> none  [the longest x1 19.6 us: on_device(): act = jax.nn.silu(total + offset).astype(jnp.bfloat16)]
    slice x11 -> x0, local copies, waits for them, and re-layouts: 24.4 us -> none  [the longest x1 8.7 us: on_device(): x_part = conv_input[:, :x_width].reshape(rows, head_count, slab)]
    exp x19 -> x0, local copies, waits for them, and re-layouts: 17.2 us -> none  [the longest x1 16.5 us: on_device(): grown = jnp.exp(jnp.repeat(cum, HEADDIM, axis=2))]
  transfers between devices with their start and end apart: 5 -> 0, of which waited for: 3 -> 0; matrix products, arithmetic and copies ran while one was open for 10% -> 0% of each run, Pallas kernels for 0% -> 0%
where the time goes in v1:
time: 268 us; the launch traced here: 267 us
  Pallas kernels  257 us (96%)
  local copies, waits for them, and re-layouts  9.24 us (3%)
    pallas_call x1, Pallas kernels, on_device(): pl.pallas_call(functools.partial(kernel, n_ctx, n_head), out_shape=jax.Sh...  257 us
    unnamed x1, local copies, waits for them, and re-layouts  8.44 us

profile of v1, /device:TPU:23, one launch (start us, length us, event | category | flops | bytes accessed | tf_op | source)
XLA Modules:
  0.0 267.3 jit_solution(2469000860322762640)
XLA Ops:
  0.0 0.7 pad_maximum_fusion
  0.7 0.8 copy.11.head_ref
  1.5 257.4 %shard_map.73 = bf16[2048,2048]{1,0:T(8,128)(2,1)} custom-call(bf16[256,20480]{1,0:T(8,128)(2,1)} %x_hbm.1, bf16[256,256]{1,0:T(8,128)(2,1)} %dt_ref.1, bf16[4,20480]{1,0:T(4,128)(2,1)} %w_ref.1, f32[1,20480]{1,0:T(1,128)} %bitcast.4, f32[256,3]{1,0:T(8,128)} %copy.11.head_ref), custom_call_target="tpu_custom_call" | custom-call | tf_op jit(solution)/shard_map/pallas_call | solution.py:396
  258.9 8.4 %copy.13 = bf16[2048,2048]{1,0:T(8,128)(2,1)} copy(bf16[2048,2048]{1,0:T(8,128)(2,1)} %shard_map.73) | data formatting | bytes 16777216

commit v2 on v1

--- a/solution.py
+++ b/solution.py
@@ -15,7 +15,7 @@
 CHUNK = 128
 UNIT = 256
 RIM = 16
-AHEAD = 3
+AHEAD = 2
 SKIP_ROW = 126
 TOTAL_ROW = 127
 
@@ -40,9 +40,9 @@
 
 def kernel(
     n_ctx, n_head,
-    x_hbm, dt_ref, w_ref, b_ref, head_ref,
+    x_hbm, dt_ref, w_ref, b_ref, a_ref, bias_ref, skip_ref,
     out_hbm,
-    buf, dts, dtr, dtf, daf, b_t, c_act, gram, feat, fade_t, fade, e_u, e_v, e_g, y_buf, state, s_out, s_in,
+    buf, heads, dts, dtr, dtf, daf, b_t, c_act, gram, feat, fade_t, fade, e_u, e_v, e_g, y_buf, state, s_out, s_in,
     send_sem, recv_sem, dt_send, dt_recv, rim_send, rim_recv, chain_send, chain_recv, out_sem,
 ):
     tok = x_hbm.shape[0]
@@ -167,13 +167,6 @@
             buf.at[pl.ds(RIM, length), place(p + 2)], out_hbm.at[:, place(p)], out_sem.at[p]
         )
 
-    dts[...] = dt_ref[...].astype(F32).T.astype(BF16)
-
-    @pl.when(ctx == 0)
-    def _():
-        buf[0:RIM, :] = jnp.zeros((RIM, buf.shape[1]), BF16)
-        s_in[...] = jnp.zeros(s_in.shape, F32)
-
     has_next = (ctx < n_ctx - 1).astype(jnp.int32)
     has_prev = (ctx > 0).astype(jnp.int32)
     is_last = (me == last).astype(jnp.int32)
@@ -181,6 +174,9 @@
         barrier, last + has_next * (1 + last * is_last) + has_prev * (2 - is_last)
     )
 
+    unit_start(0)
+    unit_start(1)
+    dts[...] = dt_ref[...].astype(F32).T.astype(BF16)
     for d in turns:
         dt_copy(lax.rem(me + d, n_head)).start()
     own_dt = pltpu.make_async_copy(
@@ -198,16 +194,23 @@
             for j in range(n_head):
                 rim_copy(part, j).start()
 
-    unit_start(0)
-    unit_start(1)
     for p in range(min(AHEAD, pieces)):
         unit_start(p + 2)
+
+    @pl.when(ctx == 0)
+    def _():
+        buf[0:RIM, :] = jnp.zeros((RIM, buf.shape[1]), BF16)
+        s_in[...] = jnp.zeros(s_in.shape, BF16)
+
+    heads[...] = jnp.concatenate(
+        [a_ref[...], bias_ref[...], skip_ref[...], jnp.zeros((5, HEADS), F32)], 0
+    ).T
 
     for src in range(n_head):
         where = dtr.at[:, pl.ds(src * tok, tok)]
         pltpu.make_async_copy(where, where, dt_recv.at[src]).wait()
     mine = pl.ds(pl.multiple_of(me * hd, hd), hd)
-    per_head = head_ref[mine, :]
+    per_head = heads[mine, :]
     dt_now = softplus(dtr[...].astype(F32) + per_head[:, 1:2])
     dtf[...] = dt_now
     daf[...] = -jnp.exp(per_head[:, 0:1]) * dt_now
@@ -294,11 +297,10 @@
         def _():
             pltpu.make_async_copy(s_in.at[p], s_in.at[p], chain_recv.at[p]).wait()
 
-        slot = lax.rem(p, 2)
-
-        @pl.when(jnp.logical_and(ctx > 0, ctx < n_ctx - 1))
+        @pl.when(ctx < n_ctx - 1)
         def _():
-            s_out[p] = fade[slot, TOTAL_ROW : TOTAL_ROW + 1, :] * s_in[p] + s_out[p]
+            before = s_in[p].astype(F32)
+            s_out[p] = (fade[TOTAL_ROW : TOTAL_ROW + 1, :] * before + state[...]).astype(BF16)
             chain_copy(p).start()
 
         e_g[...] = spread(p, 4)
@@ -306,9 +308,9 @@
         def block(i, _):
             rows = pl.ds(pl.multiple_of(i * tok, tok), tok)
             grown = dot(feat[rows, :], e_g[...])
-            late = grown * dot(c_act[rows, :], s_in[p].astype(BF16))
+            late = grown * dot(c_act[rows, :], s_in[p])
             buf[pl.ds(pl.multiple_of(RIM + i * tok, RIM), tok), place(p + 2)] = (
-                y_buf[slot, rows, :] + late
+                y_buf[rows, :] + late
             ).astype(BF16)
             return 0
 
@@ -322,11 +324,10 @@
         def _():
             unit_start(p + AHEAD + 2)
 
-        slot = lax.rem(p, 2)
         e_u[...] = spread(p, 0)
         e_v[...] = spread(p, 2)
         expand = jnp.where(row[0:hd] == col[0:hd] + p * per_unit, 1.0, 0.0)
-        fade[slot] = dot(fade_t[...], expand, lax.Precision.HIGHEST)
+        fade[...] = dot(fade_t[...], expand, lax.Precision.HIGHEST)
         state[...] = jnp.zeros(state.shape, F32)
 
         def block(src, _):
@@ -340,29 +341,19 @@
                 span = pl.ds(pl.multiple_of(src * tok + i * CHUNK, CHUNK), CHUNK)
                 entering = state[...]
                 y = dot(gram[span, :], scaled[part]) + dot(c_act[span, :], entering.astype(BF16))
-                y_buf[slot, span, :] = (
-                    grow[part] * y + fade[slot, SKIP_ROW : SKIP_ROW + 1, :] * act[part]
+                y_buf[span, :] = (
+                    grow[part] * y + fade[SKIP_ROW : SKIP_ROW + 1, :] * act[part]
                 )
                 added = dot(b_t[:, span], scaled[part])
                 k = src * (tok // CHUNK) + i
-                state[...] = fade[slot, pl.ds(k, 1), :] * (entering + added)
+                state[...] = fade[pl.ds(k, 1), :] * (entering + added)
             return 0
 
         lax.fori_loop(0, n_head, block, 0)
-        s_out[p] = state[...]
-
-        @pl.when(ctx == 0)
-        def _():
-            chain_copy(p).start()
-
-        @pl.when(p > 0)
-        def _():
-            finish(p - 1)
-
+        finish(p)
         return 0
 
     lax.fori_loop(0, pieces, piece, 0)
-    finish(pieces - 1)
 
     for d in turns:
         dt_copy(lax.rem(me + d, n_head)).wait_send()
@@ -389,17 +380,17 @@
     slab = HEADS * HEADDIM // n_head
     hd = HEADS // n_head
     pieces = slab // UNIT
-    per_head = jnp.stack([a_log, dt_bias, d_skip], 1)
     vmem = pl.BlockSpec(memory_space=pltpu.VMEM)
     anywhere = pl.BlockSpec(memory_space=pl.ANY)
     dma = pltpu.SemaphoreType.DMA
     return pl.pallas_call(
         functools.partial(kernel, n_ctx, n_head),
         out_shape=jax.ShapeDtypeStruct((length, slab), BF16),
-        in_specs=[anywhere, vmem, vmem, vmem, vmem],
+        in_specs=[anywhere] + [vmem] * 6,
         out_specs=anywhere,
         scratch_shapes=[
             pltpu.VMEM((RIM + length, slab + 2 * STATE), BF16),
+            pltpu.VMEM((HEADS, 8), F32),
             pltpu.VMEM((HEADS, tok), BF16),
             pltpu.VMEM((hd, length), BF16),
             pltpu.VMEM((hd, length), F32),
@@ -409,14 +400,14 @@
             pltpu.VMEM((length, CHUNK), BF16),
             pltpu.VMEM((length, 8 * hd), BF16),
             pltpu.VMEM((128, hd), F32),
-            pltpu.VMEM((2, 128, UNIT), F32),
+            pltpu.VMEM((128, UNIT), F32),
             pltpu.VMEM((8 * hd, UNIT), BF16),
             pltpu.VMEM((8 * hd, UNIT), BF16),
             pltpu.VMEM((8 * hd, UNIT), BF16),
-            pltpu.VMEM((2, length, UNIT), F32),
+            pltpu.VMEM((length, UNIT), F32),
             pltpu.VMEM((STATE, UNIT), F32),
-            pltpu.VMEM((pieces, STATE, UNIT), F32),
-            pltpu.VMEM((pieces, STATE, UNIT), F32),
+            pltpu.VMEM((pieces, STATE, UNIT), BF16),
+            pltpu.VMEM((pieces, STATE, UNIT), BF16),
             dma((pieces + 2, n_head)),
             dma((pieces + 2, n_head)),
             dma((n_head,)),
@@ -428,9 +419,14 @@
             dma((pieces,)),
         ],
         compiler_params=pltpu.CompilerParams(
-            collective_id=0, has_side_effects=True, vmem_limit_bytes=56 * 1024 * 1024
+            collective_id=0, has_side_effects=True, vmem_limit_bytes=40 * 1024 * 1024
         ),
-    )(conv_input, dt_raw, conv_weight, conv_bias.reshape(1, -1), per_head)
+    )(
+        conv_input,
+        dt_raw,
+        conv_weight,
+        *(table.reshape(1, -1) for table in (conv_bias, a_log, dt_bias, d_skip)),
+    )
 
 
 def solution(mesh):

time: 268 us -> 272 us (1.015)
  local copies, waits for them, and re-layouts: 9.24 us -> 16.4 us
    unnamed x1 -> x15, local copies, waits for them, and re-layouts: 8.44 us -> 16.4 us
where the time goes in v2:
time: 272 us
  Pallas kernels  256 us (94%)
  local copies, waits for them, and re-layouts  16.4 us (6%)
    pallas_call x1, Pallas kernels, on_device(): pl.pallas_call(functools.partial(kernel, n_ctx, n_head), out_shape=jax.Sh...  256 us
    unnamed x15, local copies, waits for them, and re-layouts  16.4 us

profile of v2, /device:TPU:23, one launch (start us, length us, event | category | flops | bytes accessed | tf_op | source)
XLA Modules:
  0.0 272.0 jit_solution(15798527831894149358)
XLA Ops:
  0.0 0.0 copy-start.1
  0.0 0.9 copy-done.1
  0.9 0.0 copy-start.2
  0.9 0.9 copy-done.2
  1.8 0.0 copy-start.3
  1.8 0.9 copy-done.3
  2.7 0.0 copy-start.4
  2.7 0.7 copy-done.4
  3.4 0.0 copy-start.5
  3.4 0.7 copy-done.5
  4.1 0.0 copy-start.6
  4.1 0.7 copy-done.6
  4.7 255.6 %shard_map.73 = bf16[2048,2048]{1,0:T(8,128)(2,1)S(1)} custom-call(bf16[256,20480]{1,0:T(8,128)(2,1)} %x_hbm.1, bf16[256,256]{1,0:T(8,128)(2,1)S(1)} %copy-done.2, bf16[4,20480]{1,0:T(4,128)(2,1)S(1)} %copy-done.1, f32[1,20480]{1,0:T(1,128)S(1)} %bitcast.4, f32[1,256]{1,0:T(1,128)S(1)} %bitcast.5, f32[1,256]{1,0:T(1,128)S(1)} %bitcast.6, f32[1,256]{1,0:T(1,128)S(1)} %bitcast.7), custom_call_target="tpu_custom_call" | custom-call | tf_op jit(solution)/shard_map/pallas_call | solution.py:386
  260.4 0.0 copy-start
  260.4 3.2 %copy-done = bf16[2048,2048]{1,0:T(8,128)(2,1)} copy-done((bf16[2048,2048]{1,0:T(8,128)(2,1)}, bf16[2048,2048]{1,0:T(8,128)(2,1)S(1)}, u32[]{:S(2)}) %copy-start) | copy-done | bytes 8388632
  263.6 8.4 %copy.9 = bf16[2048,2048]{1,0:T(8,128)(2,1)} copy(bf16[2048,2048]{1,0:T(8,128)(2,1)} %copy-done) | data formatting | bytes 16777216
Async XLA Ops:
  0.0 0.9 copy-start.1
  0.9 0.9 copy-start.2
  1.8 0.9 copy-start.3
  2.7 0.7 copy-start.4
  3.4 0.7 copy-start.5
  4.1 0.7 copy-start.6
  260.4 3.2 %copy-start = (bf16[2048,2048]{1,0:T(8,128)(2,1)}, bf16[2048,2048]{1,0:T(8,128)(2,1)S(1)}, u32[]{:S(2)}) copy-start(bf16[2048,2048]{1,0:T(8,128)(2,1)S(1)} %shard_map.73) | copy-start | bytes 25165828

commit v3 on v2

--- a/solution.py
+++ b/solution.py
@@ -16,6 +16,7 @@
 UNIT = 256
 RIM = 16
 AHEAD = 2
+PARTS = 16
 SKIP_ROW = 126
 TOTAL_ROW = 127
 
@@ -40,10 +41,10 @@
 
 def kernel(
     n_ctx, n_head,
-    x_hbm, dt_ref, w_ref, b_ref, a_ref, bias_ref, skip_ref,
+    x_hbm, dt_hbm, w_hbm, b_hbm, a_hbm, bias_hbm, skip_hbm,
     out_hbm,
-    buf, heads, dts, dtr, dtf, daf, b_t, c_act, gram, feat, fade_t, fade, e_u, e_v, e_g, y_buf, state, s_out, s_in,
-    send_sem, recv_sem, dt_send, dt_recv, rim_send, rim_recv, chain_send, chain_recv, out_sem,
+    dt_ref, w_ref, b_ref, a_ref, bias_ref, skip_ref, buf, heads, dts, dtr, dtf, daf, b_t, c_act, gram, feat, fade_t, fade, e_u, e_v, e_g, y_buf, state, s_out, s_in,
+    send_sem, recv_sem, dt_send, dt_recv, rim_send, rim_recv, chain_send, chain_recv, out_sem, load_sem,
 ):
     tok = x_hbm.shape[0]
     length = tok * n_head
@@ -62,6 +63,22 @@
     def device(c, j):
         return (c, j)
 
+    loads = [
+        pltpu.make_async_copy(source, held, load_sem.at[i])
+        for i, (source, held) in enumerate(
+            (
+                (dt_hbm, dt_ref),
+                (w_hbm, w_ref),
+                (b_hbm, b_ref),
+                (a_hbm, a_ref),
+                (bias_hbm, bias_ref),
+                (skip_hbm, skip_ref),
+            )
+        )
+    ]
+    for load in loads:
+        load.start()
+
     barrier = pltpu.get_barrier_semaphore()
 
     def greet(c, j):
@@ -176,6 +193,8 @@
 
     unit_start(0)
     unit_start(1)
+    for load in loads:
+        load.wait()
     dts[...] = dt_ref[...].astype(F32).T.astype(BF16)
     for d in turns:
         dt_copy(lax.rem(me + d, n_head)).start()
@@ -373,6 +392,20 @@
         out_copy(p).wait()
 
 
+def hand_out(result, out_hbm, sem):
+    rows = result.shape[0] // PARTS
+    copies = [
+        pltpu.make_async_copy(
+            result.at[pl.ds(i * rows, rows), :], out_hbm.at[pl.ds(i * rows, rows), :], sem.at[i]
+        )
+        for i in range(PARTS)
+    ]
+    for copy in copies:
+        copy.start()
+    for copy in copies:
+        copy.wait()
+
+
 def on_device(conv_input, dt_raw, conv_weight, conv_bias, a_log, dt_bias, d_skip):
     n_ctx, n_head = lax.axis_size("ctx"), lax.axis_size("head")
     tok = conv_input.shape[0]
@@ -380,15 +413,20 @@
     slab = HEADS * HEADDIM // n_head
     hd = HEADS // n_head
     pieces = slab // UNIT
-    vmem = pl.BlockSpec(memory_space=pltpu.VMEM)
     anywhere = pl.BlockSpec(memory_space=pl.ANY)
     dma = pltpu.SemaphoreType.DMA
-    return pl.pallas_call(
+    result = pl.pallas_call(
         functools.partial(kernel, n_ctx, n_head),
         out_shape=jax.ShapeDtypeStruct((length, slab), BF16),
-        in_specs=[anywhere] + [vmem] * 6,
+        in_specs=[pl.BlockSpec(memory_space=pltpu.HBM)] * 7,
         out_specs=anywhere,
         scratch_shapes=[
+            pltpu.VMEM(dt_raw.shape, BF16),
+            pltpu.VMEM(conv_weight.shape, BF16),
+            pltpu.VMEM((1, conv_bias.shape[0]), F32),
+            pltpu.VMEM((1, HEADS), F32),
+            pltpu.VMEM((1, HEADS), F32),
+            pltpu.VMEM((1, HEADS), F32),
             pltpu.VMEM((RIM + length, slab + 2 * STATE), BF16),
             pltpu.VMEM((HEADS, 8), F32),
             pltpu.VMEM((HEADS, tok), BF16),
@@ -417,6 +455,7 @@
             dma((pieces,)),
             dma((pieces,)),
             dma((pieces,)),
+            dma((6,)),
         ],
         compiler_params=pltpu.CompilerParams(
             collective_id=0, has_side_effects=True, vmem_limit_bytes=40 * 1024 * 1024
@@ -429,6 +468,16 @@
     )
 
 
+    return pl.pallas_call(
+        hand_out,
+        out_shape=jax.ShapeDtypeStruct((length, slab), BF16),
+        in_specs=[anywhere],
+        out_specs=pl.BlockSpec(memory_space=pltpu.HBM),
+        scratch_shapes=[dma((PARTS,))],
+        compiler_params=pltpu.CompilerParams(vmem_limit_bytes=4 * 1024 * 1024),
+    )(result)
+
+
 def solution(mesh):
     placed = (P(("ctx", "head"), None), P(("ctx", "head"), None), P(), P(), P(), P(), P())
     return jax.shard_map(

time: 272 us -> 265 us (0.974)
  local copies, waits for them, and re-layouts: 16.4 us -> 4.74 us
  Pallas kernels: 256 us -> 260 us
    unnamed x15 -> x12, local copies, waits for them, and re-layouts: 16.4 us -> 4.74 us
    pallas_call x0 -> x1, Pallas kernels: none -> 3.42 us  [on_device(): pl.pallas_call(hand_out, out_shape=jax.ShapeDtypeStruct((length, slab), B...]
where the time goes in v3:
time: 265 us
  Pallas kernels  260 us (98%)
  local copies, waits for them, and re-layouts  4.74 us (2%)
    pallas_call x1, Pallas kernels, on_device(): pl.pallas_call(functools.partial(kernel, n_ctx, n_head), out_shape=jax.Sh...  257 us

profile of v3, /device:TPU:23, one launch (start us, length us, event | category | flops | bytes accessed | tf_op | source)
XLA Modules:
  0.0 264.9 jit_solution(2080830956015222238)
XLA Ops:
  0.0 0.0 copy-start
  0.0 0.9 copy-done
  0.9 0.0 copy-start.1
  0.9 0.9 copy-done.1
  1.8 0.0 copy-start.2
  1.8 0.9 copy-done.2
  2.7 0.0 copy-start.3
  2.7 0.7 copy-done.3
  3.4 0.0 copy-start.4
  3.4 0.7 copy-done.4
  4.1 0.0 copy-start.5
  4.1 0.7 copy-done.5
  4.7 256.7 %shard_map.73.result = bf16[2048,2048]{1,0:T(8,128)(2,1)S(1)} custom-call(bf16[256,20480]{1,0:T(8,128)(2,1)} %x_hbm.1, bf16[256,256]{1,0:T(8,128)(2,1)S(1)} %copy-done.1, bf16[4,20480]{1,0:T(4,128)(2,1)S(1)} %copy-done, f32[1,20480]{1,0:T(1,128)S(1)} %bitcast.4, f32[1,256]{1,0:T(1,128)S(1)} %bitcast.5, f32[1,256]{1,0:T(1,128)S(1)} %bitcast.6, ...), custom_call_target="tpu_custom_call" | custom-call | tf_op jit(solution)/shard_map/pallas_call | solution.py:418
  261.5 3.4 %shard_map.74 = bf16[2048,2048]{1,0:T(8,128)(2,1)} custom-call(bf16[2048,2048]{1,0:T(8,128)(2,1)S(1)} %shard_map.73.result), custom_call_target="tpu_custom_call" | custom-call | tf_op jit(solution)/shard_map/pallas_call | solution.py:471
Async XLA Ops:
  0.0 0.9 copy-start
  0.9 0.9 copy-start.1
  1.8 0.9 copy-start.2
  2.7 0.7 copy-start.3
  3.4 0.7 copy-start.4
  4.1 0.7 copy-start.5
